TPU v7x, 32 devices: a whole 2x2x4 slice. The times are simulated.
32 devices in a mesh: dp: 2 (over x), row: 4 (over z), col: 4 (over y, core).
Axes of the slice: x: 2, y: 2, z: 4, core: 2. Of those that a mesh axis runs over, the one named last changes fastest.
Arguments:
- activations: bfloat16 [512, 7424], P('col', ('dp', 'row')), may hold values from -6 to 6
- upstream: bfloat16 [512, 29696], P(('dp', 'row'), 'col'), may hold values from -0.375 to 0.375
- weight: bfloat16 [7424, 29696], P(('dp', 'row'), 'col'), may hold values from -0.75 to 0.75
- bin_fill: int32 [8], P(('dp', 'row')), may hold values from 16 to 64, as said below
Outputs:
- d_input: bfloat16 [512, 7424], P('col', ('dp', 'row'))
- d_weight: bfloat16 [7424, 29696], P(('dp', 'row'), 'col')
Inputs may be any that keep to these rules, and one draw needn't show every extreme that they name: `bin_fill`: in every draw some bin is full, with 64 tokens, and some bin holds 16 tokens.
All inputs are finite; a program needn't handle non-finite values.
Results may differ from a plain program's by a relative error of at most 0.001.
Values may be sent and summed in bfloat16 or wider, within the bound.
A program may use at most 64 MiB of HBM per device.

v0:
```python
import jax
import jax.numpy as jnp
from jax import lax
from jax.sharding import PartitionSpec as P


def on_device(activations, upstream, weight, bin_fill):
    row_count = upstream.shape[0]
    slot_index = jnp.arange(row_count, dtype=jnp.int32)
    live_rows = slot_index < bin_fill[0]
    masked = jnp.where(live_rows[:, None], upstream, jnp.zeros_like(upstream))
    all_inputs = lax.all_gather(activations, "col", axis=0, tiled=True)
    block_rows = lax.all_gather(masked, ("dp", "row"), axis=0, tiled=True)
    grad_w = lax.dot_general(
        all_inputs, block_rows, (((0,), (0,)), ((), ())), preferred_element_type=jnp.float32
    )
    partial_value = lax.dot_general(
        block_rows, weight, (((1,), (1,)), ((), ())), preferred_element_type=jnp.float32
    )
    grad_x = partial_value
    grad_w, grad_x = (grad_w, grad_x)
    d_input = lax.psum_scatter(grad_x, "col", scatter_dimension=0, tiled=True).astype(jnp.bfloat16)
    return (d_input, grad_w.astype(jnp.bfloat16))


def solution(mesh):
    in_specs = (
        P("col", ("dp", "row")),
        P(("dp", "row"), "col"),
        P(("dp", "row"), "col"),
        P(("dp", "row")),
    )
    out_specs = (P("col", ("dp", "row")), P(("dp", "row"), "col"))
    return jax.shard_map(
        on_device, mesh=mesh, in_specs=in_specs, out_specs=out_specs, check_vma=False
    )
```

profile of v0, /device:TPU:1, one launch (start us, length us, event | category | flops | bytes accessed | tf_op | source)
XLA Modules:
  0.0 178.8 jit_solution(18442519951073731675)
XLA Ops:
  7.2 0.0 all-gather.2.cloned.1.call-start
  7.9 2.3 %broadcast_select_fusion = bf16[64,7424]{1,0:T(8,128)(2,1)} fusion(bf16[64,7424]{1,0:T(8,128)(2,1)} %param.5, pred[64]{0:T(512)(128)(4,1)S(1)} %iota_compare_fusion), kind=kLoop, calls=%fused_computation.2 | loop fusion | flops 475136 | bytes 1900608 | tf_op jit(solution)/shard_map/jit(_where)/select_n | solution.py:11
  10.1 0.0 all-gather.2.cloned.1.call-update
  10.2 0.0 copy-start
  10.2 0.0 reduce-scatter.2.cloned.1.call-start
  10.2 117.4 %all-gather.2.cloned.1.call-done = bf16[512,7424]{1,0:T(8,128)(2,1)} async-done(((bf16[64,7424]{1,0:T(8,128)(2,1)}), bf16[512,7424]{1,0:T(8,128)(2,1)}) %all-gather.2.cloned.1.call-update) | async-done | bytes 7602192 | tf_op jit(solution)/shard_map/all_gather | solution.py:13
  127.6 13.6 %fusion.1 = f32[512,928]{0,1:T(8,128)} fusion(bf16[512,7424]{1,0:T(8,128)(2,1)} %all-gather.2.cloned.1.call-done, bf16[928,7424]{1,0:T(8,128)(2,1)} %param.6), kind=kOutput, calls=%fused_computation.4 | convolution fusion | flops 7054819328 | bytes 23281664 | tf_op jit(solution)/shard_map/dot_general | solution.py:17
  141.2 0.0 reduce-scatter.2.cloned.1.call-update
  141.3 0.0 copy-done
  141.3 10.4 %all_gather.7 = bf16[512,928]{0,1:T(8,128)(2,1)S(1)} all-gather(bf16[128,928]{0,1:T(8,128)(2,1)S(1)} %copy-done), channel_id=1, replica_groups=mesh['dp'=2,'row'=4,'col'=4] {'col'}, dimensions={0}, use_global_device_ids=true | all-gather | bytes 1187840 | tf_op jit(solution)/shard_map/all_gather | solution.py:12
  151.7 13.6 %fusion = bf16[928,7424]{1,0:T(8,128)(2,1)} fusion(bf16[512,928]{0,1:T(8,128)(2,1)S(1)} %all_gather.7, bf16[512,7424]{1,0:T(8,128)(2,1)} %all-gather.2.cloned.1.call-done), kind=kOutput, calls=%fused_computation.1 | convolution fusion | flops 7061708800 | bytes 22331392 | tf_op jit(solution)/shard_map/dot_general | solution.py:14
  165.2 5.0 %reduce-scatter.2.cloned.1.call-done = f32[128,928]{0,1:T(8,128)} async-done(((f32[512,928]{0,1:T(8,128)}), f32[128,928]{0,1:T(8,128)}) %reduce-scatter.2.cloned.1.call-update) | async-done | bytes 475152 | tf_op jit(solution)/shard_map/reduce_scatter | solution.py:22
  170.3 1.7 convert_element_type.9
  (1 shorter events, 0.0 us)
Async XLA Ops:
  7.2 120.4 %all-gather.2.cloned.1.call-start = ((), (), s32[]{:S(2)}) async-start(), calls=%async_computation.1 | async-start | bytes 8552448 | tf_op jit(solution)/shard_map/all_gather | solution.py:13
  10.2 131.1 %copy-start = (bf16[128,928]{0,1:T(8,128)(2,1)S(1)}, bf16[128,928]{0,1:T(8,128)(2,1)}, u32[]{:S(2)}) copy-start(bf16[128,928]{0,1:T(8,128)(2,1)} %param.4) | copy-start | bytes 712708
  10.2 160.1 %reduce-scatter.2.cloned.1.call-start = ((), (), s32[]{:S(2)}) async-start(), calls=%async_computation.2 | async-start | bytes 2375680 | tf_op jit(solution)/shard_map/reduce_scatter | solution.py:22
Sparse Core Ops, SparseCore 0:
  10.7 116.8 all-gather.1
  141.4 28.8 reduce-scatter.1
where the time goes:
time: 180 us; the launch traced here: 179 us
  waiting for transfers between devices  122 us (68%)
  matrix products  27.2 us (15%)
  between operations  14.7 us (8%)
  blocking collectives  10.4 us (6%)
  other arithmetic  4 us (2%)
    all_gather x1, waiting for transfers between devices, on_device(): block_rows = lax.all_gather(masked, ('dp', 'row'), axis=0, tiled=True)  117 us
    dot_general x1, matrix products, on_device(): lax.dot_general(block_rows, weight, (((1,), (1,)), ((), ())), preferred_e...  13.6 us
    dot_general x1, matrix products, on_device(): lax.dot_general(all_inputs, block_rows, (((0,), (0,)), ((), ())), preferr...  13.6 us
    all_gather x1, blocking collectives, on_device(): all_inputs = lax.all_gather(activations, 'col', axis=0, tiled=True)  10.4 us
    reduce_scatter x1, waiting for transfers between devices, on_device(): lax.psum_scatter(grad_x, 'col', scatter_dimension=0, tiled=True)  5.02 us
  transfers between devices with their start and end apart: 2, of which 2 were waited for; matrix products, arithmetic and copies ran while one was open for 8% of the time, Pallas kernels for 0%

commit v1 on v0

v1 whole, which is shorter than its diff:
```python
import functools

import jax
import jax.numpy as jnp
from jax import lax
from jax.experimental import pallas as pl
from jax.experimental.pallas import tpu as pltpu
from jax.sharding import PartitionSpec as P

MESH = pl.DeviceIdType.MESH
ROWS = 16
STEPS = 14


def own(plane, order=(0, 1, 2, 3)):
    return [(plane, 0, quarter) for quarter in order]


def other(plane, order=(0, 1, 2, 3)):
    return [(plane, 1, quarter) for quarter in order]


END = {
    "x": own(0) + own(1) + own(2) + own(3, (0, 1)),
    "in": own(0) + other(0),
}
MIDDLE = {
    "x": own(1) + own(2) + own(3, (2, 3, 0, 1)),
    "in": own(1) + own(0),
    "out": own(1) + own(2) + own(3) + other(3, (2, 3)),
}
LINKS = ("x", "in", "out")
ORDER = ((0, 1, 2, 3), (1, 0, 2, 3))


def gather_kernel(
    up_ref, fill_ref, act_ref, w_ref, g_out, act_t_out, din_out,
    gv, wv, av, acc, parts, piece_in, piece_out, act_in, act_sent,
    part_in, part_sent, w_sem, g_sem,
):
    x, z, c = lax.axis_index("dp"), lax.axis_index("row"), lax.axis_index("col")
    side = z // 2
    is_end = (z == 0) | (z == 3)
    is_middle = (z == 1) | (z == 2)
    inward, outward = z + 1 - 2 * side, z - 1 + 2 * side
    targets = {"x": {"dp": 1 - x}, "in": {"row": inward}, "out": {"row": outward}}
    peers = [{"col": lax.rem(c + k, 4)} for k in (1, 2, 3)]
    ff = gv.shape[2]
    tiles = ff // 256

    def absolute(plane):
        return plane + side * (3 - 2 * plane)

    load_w = pltpu.make_async_copy(w_ref, wv, w_sem)
    load_w.start()
    live = lax.broadcasted_iota(jnp.int32, up_ref.shape, 0) < fill_ref[0]
    here = pl.ds(pl.multiple_of(x * 64, 64), 64)
    gv[z, here, :] = jnp.where(live, up_ref[...], jnp.zeros_like(up_ref))
    av[c] = act_ref[...]

    barrier = pltpu.get_barrier_semaphore()
    for target in [targets["x"], targets["in"]] + peers:
        pl.semaphore_signal(barrier, inc=1, device_id=target, device_id_type=MESH)

    @pl.when(is_middle)
    def _():
        pl.semaphore_signal(barrier, inc=1, device_id=targets["out"], device_id_type=MESH)
        pl.semaphore_wait(barrier, 6)

    @pl.when(is_end)
    def _():
        pl.semaphore_wait(barrier, 5)

    def piece_copy(piece, link, step):
        plane, from_other, quarter = piece
        xs = 1 - x if from_other else x
        rows = pl.ds(pl.multiple_of(xs * 64 + quarter * ROWS, ROWS), ROWS)
        ref = gv.at[absolute(plane), rows, :]
        return pltpu.make_async_remote_copy(
            src_ref=ref, dst_ref=ref,
            send_sem=piece_out.at[LINKS.index(link), step],
            recv_sem=piece_in.at[absolute(plane), xs * 4 + quarter],
            device_id=targets[link], device_id_type=MESH,
        )

    arrived = [set(own(0)), set(own(1))]

    def need(role, piece):
        if piece not in arrived[role]:
            arrived[role].add(piece)
            piece_copy(piece, "x", 0).wait_recv()

    def send_step(role, step):
        queues = (END, MIDDLE)[role]
        for link, queue in queues.items():
            if 2 <= step < len(queue) + 2:
                piece_copy(queue[step - 2], link, step - 2).wait_send()
            if step < len(queue):
                need(role, queue[step])
                piece_copy(queue[step], link, step).start()

    def each_role(do):
        pl.when(is_end)(lambda: do(0))
        pl.when(is_middle)(lambda: do(1))

    def lump_plane(lump):
        first, second = ORDER[0][lump], ORDER[1][lump]
        return absolute(jnp.where(is_end, first, second))

    def bin_copy(plane, xs):
        return pltpu.make_async_copy(
            gv.at[plane, pl.ds(xs * 64, 64), :],
            g_out.at[pl.ds(pl.multiple_of((xs * 4 + plane) * 64, 64), 64), :],
            g_sem.at[plane, xs],
        )

    def prepare(lump):
        def wait_all(role):
            plane = ORDER[role][lump]
            for piece in own(plane) + other(plane):
                need(role, piece)

        each_role(wait_all)
        plane = lump_plane(lump)
        for xs in range(2):
            bin_copy(plane, xs).start()
        acc[plane] = jnp.zeros_like(acc[plane])

    def multiply(lump, low, high):
        plane = lump_plane(lump)

        def body(k, carry):
            cols = pl.ds(pl.multiple_of(k * 256, 256), 256)
            acc[plane] += lax.dot_general(
                gv[plane, :, cols], wv[:, cols], (((1,), (1,)), ((), ())),
                preferred_element_type=jnp.float32,
            )
            return carry

        lax.fori_loop(low, high, body, 0)

    def part_copy(plane, xs):
        owner = xs * 2 + plane // 2
        apart = lax.rem(c - owner + 4, 4)
        slot = jnp.maximum(apart - 1, 0)
        copy = pltpu.make_async_remote_copy(
            src_ref=acc.at[plane, pl.ds(xs * 64, 64), :],
            dst_ref=parts.at[slot, lax.rem(plane, 2)],
            send_sem=part_sent.at[plane, xs],
            recv_sem=part_in.at[slot, lax.rem(plane, 2)],
            device_id={"col": owner}, device_id_type=MESH,
        )
        return apart != 0, copy

    def send_parts(lump):
        for xs in range(2):
            remote, copy = part_copy(lump_plane(lump), xs)
            pl.when(remote)(copy.start)

    def act_copy(k):
        return pltpu.make_async_remote_copy(
            src_ref=av.at[c], dst_ref=av.at[c],
            send_sem=act_sent.at[k], recv_sem=act_in.at[k],
            device_id=peers[k], device_id_type=MESH,
        )

    cut = [0] + [(tiles * i) // 4 for i in (1, 2, 3)] + [tiles]
    for step in range(STEPS):
        each_role(functools.partial(lambda step, role: send_step(role, step), step))
        if step == 0:
            for k in range(3):
                act_copy(k).start()
        if step == 3:
            for k in range(3):
                act_copy(k).wait()
            for k in range(4):
                act_t_out[:, k * 128:(k + 1) * 128] = av[k].T
            load_w.wait()
        if step in (5, 9, 13):
            prepare((step - 5) // 4)
        if 5 <= step < 13:
            lump, slice_of = (step - 5) // 4, (step - 5) % 4
            multiply(lump, cut[slice_of], cut[slice_of + 1])
            if slice_of == 3:
                send_parts(lump)
        if step == 13:
            multiply(2, 0, cut[2])
    multiply(2, cut[2], tiles)
    send_parts(2)
    prepare(3)
    multiply(3, 0, tiles)
    send_parts(3)
    for step in (STEPS, STEPS + 1):
        each_role(functools.partial(lambda step, role: send_step(role, step), step))
    for par in range(2):
        plane = 2 * lax.rem(c, 2) + par
        total = acc[plane, pl.ds(pl.multiple_of((c // 2) * 64, 64), 64), :]
        for k in range(3):
            pltpu.make_async_remote_copy(
                src_ref=parts.at[k, par], dst_ref=parts.at[k, par],
                send_sem=part_sent.at[0, 0], recv_sem=part_in.at[k, par],
                device_id=peers[k], device_id_type=MESH,
            ).wait_recv()
            total += parts[k, par]
        din_out[par * 64:(par + 1) * 64, :] = total.astype(din_out.dtype)
    for plane in range(4):
        for xs in range(2):
            remote, copy = part_copy(plane, xs)
            pl.when(remote)(copy.wait_send)
            bin_copy(plane, xs).wait()


def weight_kernel(act_ref, g_ref, out_ref):
    for k in range(g_ref.shape[1] // 256):
        cols = slice(k * 256, (k + 1) * 256)
        out_ref[:, cols] = jnp.dot(
            act_ref[...], g_ref[:, cols], preferred_element_type=jnp.float32
        ).astype(out_ref.dtype)


def fused(activations, upstream, weight, bin_fill):
    d, ff = weight.shape
    tokens = upstream.shape[0] * 8
    vmem = pl.BlockSpec(memory_space=pltpu.VMEM)
    hbm = pl.BlockSpec(memory_space=pl.ANY)
    dma = pltpu.SemaphoreType.DMA
    bf16, f32 = jnp.bfloat16, jnp.float32
    gathered, act_t, d_input = pl.pallas_call(
        gather_kernel,
        out_shape=(
            jax.ShapeDtypeStruct((tokens, ff), bf16),
            jax.ShapeDtypeStruct((d, tokens), bf16),
            jax.ShapeDtypeStruct((128, d), bf16),
        ),
        in_specs=[vmem, pl.BlockSpec(memory_space=pltpu.SMEM), vmem, hbm],
        out_specs=(hbm, vmem, vmem),
        scratch_shapes=[
            pltpu.VMEM((4, 128, ff), bf16),
            pltpu.VMEM((d, ff), bf16),
            pltpu.VMEM((4, 128, d), bf16),
            pltpu.VMEM((4, 128, d), f32),
            pltpu.VMEM((3, 2, 64, d), f32),
            dma((4, 8)), dma((3, STEPS)), dma((3,)), dma((3,)),
            dma((3, 2)), dma((4, 2)), dma, dma((4, 2)),
        ],
        compiler_params=pltpu.CompilerParams(
            collective_id=0, has_side_effects=True, vmem_limit_bytes=44 * 2**20
        ),
        cost_estimate=pl.CostEstimate(
            flops=2 * tokens * ff * d, bytes_accessed=2 * ff * (d + tokens), transcendentals=0
        ),
    )(upstream, bin_fill, activations, weight)
    tile = 1024
    d_weight = pl.pallas_call(
        weight_kernel,
        out_shape=jax.ShapeDtypeStruct((d, ff), bf16),
        grid=(pl.cdiv(ff, tile),),
        in_specs=[
            pl.BlockSpec((d, tokens), lambda i: (0, 0)),
            pl.BlockSpec((tokens, tile), lambda i: (0, i)),
        ],
        out_specs=pl.BlockSpec((d, tile), lambda i: (0, i)),
        compiler_params=pltpu.CompilerParams(vmem_limit_bytes=40 * 2**20),
        cost_estimate=pl.CostEstimate(
            flops=2 * tokens * ff * d, bytes_accessed=2 * ff * (d + tokens), transcendentals=0
        ),
    )(act_t, gathered)
    return d_input, d_weight


def plain(activations, upstream, weight, bin_fill):
    live_rows = jnp.arange(upstream.shape[0], dtype=jnp.int32) < bin_fill[0]
    masked = jnp.where(live_rows[:, None], upstream, jnp.zeros_like(upstream))
    all_inputs = lax.all_gather(activations, "col", axis=0, tiled=True)
    block_rows = lax.all_gather(masked, ("dp", "row"), axis=0, tiled=True)
    grad_w = lax.dot_general(
        all_inputs, block_rows, (((0,), (0,)), ((), ())), preferred_element_type=jnp.float32
    )
    grad_x = lax.dot_general(
        block_rows, weight, (((1,), (1,)), ((), ())), preferred_element_type=jnp.float32
    )
    d_input = lax.psum_scatter(grad_x, "col", scatter_dimension=0, tiled=True)
    return d_input.astype(jnp.bfloat16), grad_w.astype(jnp.bfloat16)


def solution(mesh):
    sizes = tuple(mesh.shape[name] for name in ("dp", "row", "col"))
    in_specs = (
        P("col", ("dp", "row")),
        P(("dp", "row"), "col"),
        P(("dp", "row"), "col"),
        P(("dp", "row")),
    )
    out_specs = (P("col", ("dp", "row")), P(("dp", "row"), "col"))
    return jax.shard_map(
        fused if sizes == (2, 4, 4) else plain,
        mesh=mesh, in_specs=in_specs, out_specs=out_specs, check_vma=False,
    )
```

time: 180 us -> 115 us (0.64)
  waiting for transfers between devices: 122 us -> 0 us
  Pallas kernels: 0 us -> 104 us
  matrix products: 27.2 us -> 0 us
  between operations: 14.7 us -> 1.31 us
  blocking collectives: 10.4 us -> 0 us
  local copies, waits for them, and re-layouts: 0.01 us -> 9.38 us
  other arithmetic: 4 us -> 0 us
    all_gather x1 -> x0, waiting for transfers between devices: 117 us -> none  [on_device(): block_rows = lax.all_gather(masked, ('dp', 'row'), axis=0, tiled=True)]
    pallas_call x0 -> x2, Pallas kernels: none -> 104 us  [the longest x1 93.1 us: fused(): pl.pallas_call(gather_kernel, out_shape=(jax.ShapeDtypeStruct((tokens, ff...]
    dot_general x2 -> x0, matrix products: 27.2 us -> none  [the longest x1 13.6 us: on_device(): lax.dot_general(block_rows, weight, (((1,), (1,)), ((), ())), preferred_e...]
    all_gather x1 -> x0, blocking collectives: 10.4 us -> none  [on_device(): all_inputs = lax.all_gather(activations, 'col', axis=0, tiled=True)]
    unnamed x2 -> x8, local copies, waits for them, and re-layouts: 0.01 us -> 9.38 us
    reduce_scatter x1 -> x0, waiting for transfers between devices: 5.02 us -> none  [on_device(): lax.psum_scatter(grad_x, 'col', scatter_dimension=0, tiled=True)]
    select_n x1 -> x0, other arithmetic: 2.26 us -> none  [on_device(): masked = jnp.where(live_rows[:, None], upstream, jnp.zeros_like(upstream))]
  transfers between devices with their start and end apart: 2 -> 0, of which waited for: 2 -> 0; matrix products, arithmetic and copies ran while one was open for 8% -> 0% of each run, Pallas kernels for 0% -> 0%
where the time goes in v1:
time: 115 us
  Pallas kernels  104 us (90%)
  local copies, waits for them, and re-layouts  9.38 us (8%)
  between operations  1.31 us (1%)
    pallas_call x1, Pallas kernels, fused(): pl.pallas_call(gather_kernel, out_shape=(jax.ShapeDtypeStruct((tokens, ff...  93.1 us
    pallas_call x1, Pallas kernels, fused(): pl.pallas_call(weight_kernel, out_shape=jax.ShapeDtypeStruct((d, ff), bf1...  11.2 us
    unnamed x8, local copies, waits for them, and re-layouts  9.38 us

profile of v1, /device:TPU:1, one launch (start us, length us, event | category | flops | bytes accessed | tf_op | source)
XLA Modules:
  0.0 115.0 jit_solution(2977329399830931012)
XLA Ops:
  1.3 1.1 copy.6.act_ref
  2.4 0.0 copy-start
  2.4 1.2 %copy-done = bf16[64,7424]{1,0:T(8,128)(2,1)S(1)} copy-done((bf16[64,7424]{1,0:T(8,128)(2,1)S(1)}, bf16[64,7424]{1,0:T(8,128)(2,1)}, u32[]{:S(2)}) %copy-start) | copy-done | bytes 950296
  3.6 93.1 %shard_map.59 = (bf16[512,7424]{1,0:T(8,128)(2,1)S(1)}, bf16[928,512]{1,0:T(8,128)(2,1)S(1)}, bf16[128,928]{1,0:T(8,128)(2,1)S(1)}) custom-call(bf16[64,7424]{1,0:T(8,128)(2,1)S(1)} %copy-done, s32[1]{0:T(128)S(6)} %copy.8.fill_ref, bf16[128,928]{1,0:T(8,128)(2,1)S(1)} %copy.6.act_ref, bf16[928,7424]{1,0:T(8,128)(2,1)} %w_ref.1), custom_call_target="tpu_custom_call" | custom-call | flops 7054819328 | bytes 21381120 | tf_op jit(solution)/shard_map/pallas_call | solution.py:228
  96.6 0.0 copy-start.1
  96.7 3.1 %copy-done.1 = bf16[512,7424]{1,0:T(8,128)(2,1)} copy-done((bf16[512,7424]{1,0:T(8,128)(2,1)}, bf16[512,7424]{1,0:T(8,128)(2,1)S(1)}, u32[]{:S(2)}) %copy-start.1) | copy-done | bytes 7602200
  99.8 0.8 copy.7
  100.6 0.0 copy-start.2
  100.6 3.2 %copy-done.2 = bf16[512,7424]{1,0:T(8,128)(2,1)S(1)} copy-done((bf16[512,7424]{1,0:T(8,128)(2,1)S(1)}, bf16[512,7424]{1,0:T(8,128)(2,1)}, u32[]{:S(2)}) %copy-start.2) | copy-done | bytes 7602200
  103.8 11.2 %shard_map.60 = bf16[928,7424]{1,0:T(8,128)(2,1)} custom-call(bf16[928,512]{1,0:T(8,128)(2,1)S(1)} %get-tuple-element.6.act_ref, bf16[512,7424]{1,0:T(8,128)(2,1)S(1)} %copy-done.2), custom_call_target="tpu_custom_call" | custom-call | flops 7054819328 | bytes 21381120 | tf_op jit(solution)/shard_map/pallas_call | solution.py:254
Async XLA Ops:
  2.4 1.2 %copy-start = (bf16[64,7424]{1,0:T(8,128)(2,1)S(1)}, bf16[64,7424]{1,0:T(8,128)(2,1)}, u32[]{:S(2)}) copy-start(bf16[64,7424]{1,0:T(8,128)(2,1)} %up_ref.1) | copy-start | bytes 2850820
  96.6 3.1 %copy-start.1 = (bf16[512,7424]{1,0:T(8,128)(2,1)}, bf16[512,7424]{1,0:T(8,128)(2,1)S(1)}, u32[]{:S(2)}) copy-start(bf16[512,7424]{1,0:T(8,128)(2,1)S(1)} %get-tuple-element.7.g_ref) | copy-start | bytes 22806532
  100.6 3.2 %copy-start.2 = (bf16[512,7424]{1,0:T(8,128)(2,1)S(1)}, bf16[512,7424]{1,0:T(8,128)(2,1)}, u32[]{:S(2)}) copy-start(bf16[512,7424]{1,0:T(8,128)(2,1)} %copy-done.1) | copy-start | bytes 22806532

commit v2 on v1

--- a/solution.py
+++ b/solution.py
@@ -8,7 +8,7 @@
 from jax.sharding import PartitionSpec as P
 
 MESH = pl.DeviceIdType.MESH
-ROWS = 16
+PIECES = 4
 STEPS = 14
 
 
@@ -35,8 +35,8 @@
 
 def gather_kernel(
     up_ref, fill_ref, act_ref, w_ref, g_out, act_t_out, din_out,
-    gv, wv, av, acc, parts, piece_in, piece_out, act_in, act_sent,
-    part_in, part_sent, w_sem, g_sem,
+    gv, wv, uv, av, acc, parts, piece_in, piece_out, act_in, act_sent,
+    part_in, part_sent, w_sem, up_sem, g_sem,
 ):
     x, z, c = lax.axis_index("dp"), lax.axis_index("row"), lax.axis_index("col")
     side = z // 2
@@ -47,17 +47,15 @@
     peers = [{"col": lax.rem(c + k, 4)} for k in (1, 2, 3)]
     ff = gv.shape[2]
     tiles = ff // 256
+    cut = [tiles * i // PIECES for i in range(PIECES + 1)]
 
     def absolute(plane):
         return plane + side * (3 - 2 * plane)
 
+    load_up = pltpu.make_async_copy(up_ref, uv, up_sem)
+    load_up.start()
     load_w = pltpu.make_async_copy(w_ref, wv, w_sem)
     load_w.start()
-    live = lax.broadcasted_iota(jnp.int32, up_ref.shape, 0) < fill_ref[0]
-    here = pl.ds(pl.multiple_of(x * 64, 64), 64)
-    gv[z, here, :] = jnp.where(live, up_ref[...], jnp.zeros_like(up_ref))
-    av[c] = act_ref[...]
-
     barrier = pltpu.get_barrier_semaphore()
     for target in [targets["x"], targets["in"]] + peers:
         pl.semaphore_signal(barrier, inc=1, device_id=target, device_id_type=MESH)
@@ -65,6 +63,15 @@
     @pl.when(is_middle)
     def _():
         pl.semaphore_signal(barrier, inc=1, device_id=targets["out"], device_id_type=MESH)
+
+    av[c] = act_ref[...]
+    load_up.wait()
+    live = lax.broadcasted_iota(jnp.int32, uv.shape, 0) < fill_ref[0]
+    here = pl.ds(pl.multiple_of(x * 64, 64), 64)
+    gv[z, here, :] = jnp.where(live, uv[...], jnp.zeros_like(uv))
+
+    @pl.when(is_middle)
+    def _():
         pl.semaphore_wait(barrier, 6)
 
     @pl.when(is_end)
@@ -72,14 +79,15 @@
         pl.semaphore_wait(barrier, 5)
 
     def piece_copy(piece, link, step):
-        plane, from_other, quarter = piece
+        plane, from_other, chunk = piece
         xs = 1 - x if from_other else x
-        rows = pl.ds(pl.multiple_of(xs * 64 + quarter * ROWS, ROWS), ROWS)
-        ref = gv.at[absolute(plane), rows, :]
+        rows = pl.ds(pl.multiple_of(xs * 64, 64), 64)
+        low, high = cut[chunk] * 256, cut[chunk + 1] * 256
+        ref = gv.at[absolute(plane), rows, low:high]
         return pltpu.make_async_remote_copy(
             src_ref=ref, dst_ref=ref,
             send_sem=piece_out.at[LINKS.index(link), step],
-            recv_sem=piece_in.at[absolute(plane), xs * 4 + quarter],
+            recv_sem=piece_in.at[absolute(plane), xs * PIECES + chunk],
             device_id=targets[link], device_id_type=MESH,
         )
 
@@ -114,17 +122,18 @@
             g_sem.at[plane, xs],
         )
 
-    def prepare(lump):
-        def wait_all(role):
+    def multiply_chunk(lump, chunk):
+        def wait_chunk(role):
             plane = ORDER[role][lump]
-            for piece in own(plane) + other(plane):
-                need(role, piece)
-
-        each_role(wait_all)
-        plane = lump_plane(lump)
+            need(role, (plane, 0, chunk))
+            need(role, (plane, 1, chunk))
+
+        each_role(wait_chunk)
+        multiply(lump, cut[chunk], cut[chunk + 1])
+
+    def save_bins(lump):
         for xs in range(2):
-            bin_copy(plane, xs).start()
-        acc[plane] = jnp.zeros_like(acc[plane])
+            bin_copy(lump_plane(lump), xs).start()
 
     def multiply(lump, low, high):
         plane = lump_plane(lump)
@@ -164,34 +173,32 @@
             device_id=peers[k], device_id_type=MESH,
         )
 
-    cut = [0] + [(tiles * i) // 4 for i in (1, 2, 3)] + [tiles]
+    acc[...] = jnp.zeros_like(acc)
     for step in range(STEPS):
         each_role(functools.partial(lambda step, role: send_step(role, step), step))
         if step == 0:
             for k in range(3):
                 act_copy(k).start()
+        if step == 2:
+            load_w.wait()
         if step == 3:
             for k in range(3):
                 act_copy(k).wait()
             for k in range(4):
-                act_t_out[:, k * 128:(k + 1) * 128] = av[k].T
-            load_w.wait()
-        if step in (5, 9, 13):
-            prepare((step - 5) // 4)
-        if 5 <= step < 13:
-            lump, slice_of = (step - 5) // 4, (step - 5) % 4
-            multiply(lump, cut[slice_of], cut[slice_of + 1])
-            if slice_of == 3:
+                act_t_out[:, k * 128:(k + 1) * 128] = av[k]
+        if step >= 2:
+            lump, chunk = (step - 2) // PIECES, (step - 2) % PIECES
+            multiply_chunk(lump, chunk)
+            if chunk == PIECES - 1:
+                save_bins(lump)
                 send_parts(lump)
-        if step == 13:
-            multiply(2, 0, cut[2])
-    multiply(2, cut[2], tiles)
-    send_parts(2)
-    prepare(3)
-    multiply(3, 0, tiles)
+    for chunk in (0, 2, 1, 3):
+        multiply_chunk(3, chunk)
+    save_bins(3)
     send_parts(3)
     for step in (STEPS, STEPS + 1):
         each_role(functools.partial(lambda step, role: send_step(role, step), step))
+    totals = []
     for par in range(2):
         plane = 2 * lax.rem(c, 2) + par
         total = acc[plane, pl.ds(pl.multiple_of((c // 2) * 64, 64), 64), :]
@@ -202,7 +209,8 @@
                 device_id=peers[k], device_id_type=MESH,
             ).wait_recv()
             total += parts[k, par]
-        din_out[par * 64:(par + 1) * 64, :] = total.astype(din_out.dtype)
+        totals.append(total)
+    din_out[...] = jnp.concatenate(totals, axis=0).T.astype(din_out.dtype)
     for plane in range(4):
         for xs in range(2):
             remote, copy = part_copy(plane, xs)
@@ -210,19 +218,22 @@
             bin_copy(plane, xs).wait()
 
 
-def weight_kernel(act_ref, g_ref, out_ref):
-    for k in range(g_ref.shape[1] // 256):
-        cols = slice(k * 256, (k + 1) * 256)
-        out_ref[:, cols] = jnp.dot(
-            act_ref[...], g_ref[:, cols], preferred_element_type=jnp.float32
-        ).astype(out_ref.dtype)
+def weight_kernel(tiles, act_ref, g_ref, out_ref):
+    per_step = g_ref.shape[1] // 256
+    for k in range(per_step):
+        @pl.when(pl.program_id(0) * per_step + k < tiles)
+        def _():
+            cols = slice(k * 256, (k + 1) * 256)
+            out_ref[:, cols] = jnp.dot(
+                act_ref[...], g_ref[:, cols], preferred_element_type=jnp.float32
+            ).astype(out_ref.dtype)
 
 
 def fused(activations, upstream, weight, bin_fill):
     d, ff = weight.shape
     tokens = upstream.shape[0] * 8
     vmem = pl.BlockSpec(memory_space=pltpu.VMEM)
-    hbm = pl.BlockSpec(memory_space=pl.ANY)
+    hbm = pl.BlockSpec(memory_space=pltpu.HBM)
     dma = pltpu.SemaphoreType.DMA
     bf16, f32 = jnp.bfloat16, jnp.float32
     gathered, act_t, d_input = pl.pallas_call(
@@ -230,29 +241,30 @@
         out_shape=(
             jax.ShapeDtypeStruct((tokens, ff), bf16),
             jax.ShapeDtypeStruct((d, tokens), bf16),
-            jax.ShapeDtypeStruct((128, d), bf16),
+            jax.ShapeDtypeStruct((d, 128), bf16),
         ),
-        in_specs=[vmem, pl.BlockSpec(memory_space=pltpu.SMEM), vmem, hbm],
+        in_specs=[hbm, pl.BlockSpec(memory_space=pltpu.SMEM), vmem, hbm],
         out_specs=(hbm, vmem, vmem),
         scratch_shapes=[
             pltpu.VMEM((4, 128, ff), bf16),
             pltpu.VMEM((d, ff), bf16),
-            pltpu.VMEM((4, 128, d), bf16),
+            pltpu.VMEM((64, ff), bf16),
+            pltpu.VMEM((4, d, 128), bf16),
             pltpu.VMEM((4, 128, d), f32),
             pltpu.VMEM((3, 2, 64, d), f32),
-            dma((4, 8)), dma((3, STEPS)), dma((3,)), dma((3,)),
-            dma((3, 2)), dma((4, 2)), dma, dma((4, 2)),
+            dma((4, 2 * PIECES)), dma((3, STEPS)), dma((3,)), dma((3,)),
+            dma((3, 2)), dma((4, 2)), dma, dma, dma((4, 2)),
         ],
         compiler_params=pltpu.CompilerParams(
-            collective_id=0, has_side_effects=True, vmem_limit_bytes=44 * 2**20
+            collective_id=0, has_side_effects=True, vmem_limit_bytes=60 * 2**20
         ),
         cost_estimate=pl.CostEstimate(
             flops=2 * tokens * ff * d, bytes_accessed=2 * ff * (d + tokens), transcendentals=0
         ),
-    )(upstream, bin_fill, activations, weight)
+    )(upstream, bin_fill, activations.T, weight)
     tile = 1024
     d_weight = pl.pallas_call(
-        weight_kernel,
+        functools.partial(weight_kernel, ff // 256),
         out_shape=jax.ShapeDtypeStruct((d, ff), bf16),
         grid=(pl.cdiv(ff, tile),),
         in_specs=[
@@ -260,12 +272,12 @@
             pl.BlockSpec((tokens, tile), lambda i: (0, i)),
         ],
         out_specs=pl.BlockSpec((d, tile), lambda i: (0, i)),
-        compiler_params=pltpu.CompilerParams(vmem_limit_bytes=40 * 2**20),
+        compiler_params=pltpu.CompilerParams(vmem_limit_bytes=58 * 2**20),
         cost_estimate=pl.CostEstimate(
             flops=2 * tokens * ff * d, bytes_accessed=2 * ff * (d + tokens), transcendentals=0
         ),
     )(act_t, gathered)
-    return d_input, d_weight
+    return d_input.T, d_weight
 
 
 def plain(activations, upstream, weight, bin_fill):

time: 115 us -> 108 us (0.939)
  local copies, waits for them, and re-layouts: 9.38 us -> 0.69 us
    unnamed x8 -> x3, local copies, waits for them, and re-layouts: 9.38 us -> 0.69 us
    pallas_call x1, Pallas kernels: 11.2 us -> 15.4 us  [fused(): pl.pallas_call(functools.partial(weight_kernel, ff // 256), out_shape=jax...]
    pallas_call x1, Pallas kernels: 93.1 us -> 90 us  [fused(): pl.pallas_call(gather_kernel, out_shape=(jax.ShapeDtypeStruct((tokens, ff...]
where the time goes in v2:
time: 108 us; the launch traced here: 107 us
  Pallas kernels  105 us (97%)
  between operations  1.29 us (1%)
    pallas_call x1, Pallas kernels, fused(): pl.pallas_call(gather_kernel, out_shape=(jax.ShapeDtypeStruct((tokens, ff...  90 us
    pallas_call x1, Pallas kernels, fused(): pl.pallas_call(functools.partial(weight_kernel, ff // 256), out_shape=jax...  15.4 us

profile of v2, /device:TPU:1, one launch (start us, length us, event | category | flops | bytes accessed | tf_op | source)
XLA Modules:
  0.0 107.4 jit_solution(11077008912572015109)
XLA Ops:
  1.3 90.0 %shard_map.59 = (bf16[512,7424]{1,0:T(8,128)(2,1)}, bf16[928,512]{1,0:T(8,128)(2,1)}, bf16[928,128]{1,0:T(8,128)(2,1)}) custom-call(bf16[64,7424]{1,0:T(8,128)(2,1)} %up_ref.1, s32[1]{0:T(128)S(6)} %copy.7.fill_ref, bf16[928,128]{1,0:T(8,128)(2,1)} %bitcast.3, bf16[928,7424]{1,0:T(8,128)(2,1)} %w_ref.1), custom_call_target="tpu_custom_call" | custom-call | flops 7054819328 | bytes 21381120 | tf_op jit(solution)/shard_map/pallas_call | solution.py:239
  91.3 0.0 copy-start
  91.3 15.4 %shard_map.60 = bf16[928,7424]{1,0:T(8,128)(2,1)} custom-call(bf16[928,512]{1,0:T(8,128)(2,1)} %get-tuple-element.6.act_ref, bf16[512,7424]{1,0:T(8,128)(2,1)} %get-tuple-element.7.g_ref), custom_call_target="tpu_custom_call" | custom-call | flops 7054819328 | bytes 21381120 | tf_op jit(solution)/shard_map/pallas_call | solution.py:266
  106.7 0.0 copy-done
  106.7 0.7 copy.8
Async XLA Ops:
  91.3 15.4 %copy-start = (bf16[928,128]{1,0:T(8,128)(2,1)S(1)}, bf16[928,128]{1,0:T(8,128)(2,1)}, u32[]{:S(2)}) copy-start(bf16[928,128]{1,0:T(8,128)(2,1)} %get-tuple-element.5) | copy-start | bytes 712708

commit v3 on v2

--- a/solution.py
+++ b/solution.py
@@ -8,35 +8,53 @@
 from jax.sharding import PartitionSpec as P
 
 MESH = pl.DeviceIdType.MESH
-PIECES = 4
-STEPS = 14
-
-
-def own(plane, order=(0, 1, 2, 3)):
-    return [(plane, 0, quarter) for quarter in order]
-
-
-def other(plane, order=(0, 1, 2, 3)):
-    return [(plane, 1, quarter) for quarter in order]
+PIECES = 8
+STEPS = 28
+WINDOW = 3
+
+
+ALL = tuple(range(PIECES))
+
+
+def own(plane, order=ALL):
+    return [(plane, 0, chunk) for chunk in order]
+
+
+def other(plane, order=ALL):
+    return [(plane, 1, chunk) for chunk in order]
 
 
 END = {
-    "x": own(0) + own(1) + own(2) + own(3, (0, 1)),
+    "x": own(0) + own(1) + own(2) + own(3, (0, 1, 2, 3)),
     "in": own(0) + other(0),
 }
 MIDDLE = {
-    "x": own(1) + own(2) + own(3, (2, 3, 0, 1)),
+    "x": own(1) + own(2) + own(3, (4, 5, 6, 7, 0, 1, 2, 3)),
     "in": own(1) + own(0),
-    "out": own(1) + own(2) + own(3) + other(3, (2, 3)),
+    "out": own(1) + own(2) + own(3, (0, 1, 2, 3))
+    + [(3, side, chunk) for chunk in (4, 5, 6, 7) for side in (0, 1)],
 }
+TAIL = (6, 2, 3, 7)
+LAST = {23: 4, 25: 5, 26: 0, 27: 1}
 LINKS = ("x", "in", "out")
 ORDER = ((0, 1, 2, 3), (1, 0, 2, 3))
 
 
+def weight_columns(act, g, out, low, high):
+    def body(k, carry):
+        cols = pl.ds(pl.multiple_of(k * 256, 256), 256)
+        out[:, cols] = jnp.dot(
+            act[...], g[:, :, cols].reshape(512, 256), preferred_element_type=jnp.float32
+        ).astype(out.dtype)
+        return carry
+
+    lax.fori_loop(low, high, body, 0)
+
+
 def gather_kernel(
-    up_ref, fill_ref, act_ref, w_ref, g_out, act_t_out, din_out,
-    gv, wv, uv, av, acc, parts, piece_in, piece_out, act_in, act_sent,
-    part_in, part_sent, w_sem, up_sem, g_sem,
+    up_ref, fill_ref, act_ref, w_ref, dw_out, g_out, act_out, din_out,
+    gv, wv, uv, av, act, dw, acc, parts, piece_in, piece_out, act_in, act_sent,
+    part_in, part_sent, w_sem, up_sem, act_sem, save_sem,
 ):
     x, z, c = lax.axis_index("dp"), lax.axis_index("row"), lax.axis_index("col")
     side = z // 2
@@ -101,8 +119,8 @@
     def send_step(role, step):
         queues = (END, MIDDLE)[role]
         for link, queue in queues.items():
-            if 2 <= step < len(queue) + 2:
-                piece_copy(queue[step - 2], link, step - 2).wait_send()
+            if WINDOW <= step < len(queue) + WINDOW:
+                piece_copy(queue[step - WINDOW], link, step - WINDOW).wait_send()
             if step < len(queue):
                 need(role, queue[step])
                 piece_copy(queue[step], link, step).start()
@@ -114,13 +132,6 @@
     def lump_plane(lump):
         first, second = ORDER[0][lump], ORDER[1][lump]
         return absolute(jnp.where(is_end, first, second))
-
-    def bin_copy(plane, xs):
-        return pltpu.make_async_copy(
-            gv.at[plane, pl.ds(xs * 64, 64), :],
-            g_out.at[pl.ds(pl.multiple_of((xs * 4 + plane) * 64, 64), 64), :],
-            g_sem.at[plane, xs],
-        )
 
     def multiply_chunk(lump, chunk):
         def wait_chunk(role):
@@ -131,9 +142,15 @@
         each_role(wait_chunk)
         multiply(lump, cut[chunk], cut[chunk + 1])
 
-    def save_bins(lump):
-        for xs in range(2):
-            bin_copy(lump_plane(lump), xs).start()
+    def save(chunk):
+        cols = slice(cut[chunk] * 256, cut[chunk + 1] * 256)
+        if chunk in TAIL:
+            src, dst = gv.at[:, :, cols], g_out.at[:, :, cols]
+        else:
+            src, dst = dw.at[:, cols], dw_out.at[:, cols]
+        return pltpu.make_async_copy(src, dst, save_sem.at[chunk])
+
+    save_act = pltpu.make_async_copy(act, act_out, act_sem)
 
     def multiply(lump, low, high):
         plane = lump_plane(lump)
@@ -184,19 +201,26 @@
         if step == 3:
             for k in range(3):
                 act_copy(k).wait()
-            for k in range(4):
-                act_t_out[:, k * 128:(k + 1) * 128] = av[k]
-        if step >= 2:
+            for plane in range(4):
+                half = slice((plane % 2) * 64, (plane % 2) * 64 + 64)
+                act[:, plane * 128:(plane + 1) * 128] = jnp.concatenate(
+                    [av[plane // 2][:, half], av[2 + plane // 2][:, half]], axis=1
+                )
+            save_act.start()
+        if 2 <= step < 2 + 3 * PIECES:
             lump, chunk = (step - 2) // PIECES, (step - 2) % PIECES
             multiply_chunk(lump, chunk)
             if chunk == PIECES - 1:
-                save_bins(lump)
                 send_parts(lump)
-    for chunk in (0, 2, 1, 3):
+        if step in LAST:
+            multiply_chunk(3, LAST[step])
+            weight_columns(act, gv, dw, cut[LAST[step]], cut[LAST[step] + 1])
+            save(LAST[step]).start()
+    for chunk in TAIL:
         multiply_chunk(3, chunk)
-    save_bins(3)
+        save(chunk).start()
     send_parts(3)
-    for step in (STEPS, STEPS + 1):
+    for step in range(STEPS, STEPS + WINDOW):
         each_role(functools.partial(lambda step, role: send_step(role, step), step))
     totals = []
     for par in range(2):
@@ -215,18 +239,39 @@
         for xs in range(2):
             remote, copy = part_copy(plane, xs)
             pl.when(remote)(copy.wait_send)
-            bin_copy(plane, xs).wait()
-
-
-def weight_kernel(tiles, act_ref, g_ref, out_ref):
-    per_step = g_ref.shape[1] // 256
-    for k in range(per_step):
-        @pl.when(pl.program_id(0) * per_step + k < tiles)
-        def _():
-            cols = slice(k * 256, (k + 1) * 256)
-            out_ref[:, cols] = jnp.dot(
-                act_ref[...], g_ref[:, cols], preferred_element_type=jnp.float32
-            ).astype(out_ref.dtype)
+    save_act.wait()
+    for chunk in ALL:
+        save(chunk).wait()
+
+
+def weight_kernel(dw_ref, g_ref, act_ref, out_ref, act, gv, dw, act_sem, in_sem, out_sem):
+    tiles = out_ref.shape[1] // 256
+    cut = [tiles * i // PIECES for i in range(PIECES + 1)]
+    columns = [slice(cut[i] * 256, cut[i + 1] * 256) for i in ALL]
+    load_act = pltpu.make_async_copy(act_ref, act, act_sem)
+    load_act.start()
+    loads = {
+        i: pltpu.make_async_copy(g_ref.at[:, :, columns[i]], gv.at[:, :, columns[i]], in_sem.at[i])
+        for i in TAIL
+    }
+    for load in loads.values():
+        load.start()
+    saves = {
+        i: pltpu.make_async_copy(
+            (dw if i in TAIL else dw_ref).at[:, columns[i]], out_ref.at[:, columns[i]], out_sem.at[i]
+        )
+        for i in ALL
+    }
+    for i in ALL:
+        if i not in TAIL:
+            saves[i].start()
+    load_act.wait()
+    for i in TAIL:
+        loads[i].wait()
+        weight_columns(act, gv, dw, cut[i], cut[i + 1])
+        saves[i].start()
+    for i in ALL:
+        saves[i].wait()
 
 
 def fused(activations, upstream, weight, bin_fill):
@@ -236,47 +281,51 @@
     hbm = pl.BlockSpec(memory_space=pltpu.HBM)
     dma = pltpu.SemaphoreType.DMA
     bf16, f32 = jnp.bfloat16, jnp.float32
-    gathered, act_t, d_input = pl.pallas_call(
+    dw_head, gathered, act_t, d_input = pl.pallas_call(
         gather_kernel,
         out_shape=(
-            jax.ShapeDtypeStruct((tokens, ff), bf16),
+            jax.ShapeDtypeStruct((d, ff), bf16),
+            jax.ShapeDtypeStruct((4, 128, ff), bf16),
             jax.ShapeDtypeStruct((d, tokens), bf16),
             jax.ShapeDtypeStruct((d, 128), bf16),
         ),
         in_specs=[hbm, pl.BlockSpec(memory_space=pltpu.SMEM), vmem, hbm],
-        out_specs=(hbm, vmem, vmem),
+        out_specs=(hbm, hbm, hbm, vmem),
         scratch_shapes=[
             pltpu.VMEM((4, 128, ff), bf16),
             pltpu.VMEM((d, ff), bf16),
             pltpu.VMEM((64, ff), bf16),
             pltpu.VMEM((4, d, 128), bf16),
+            pltpu.VMEM((d, tokens), bf16),
+            pltpu.VMEM((d, ff), bf16),
             pltpu.VMEM((4, 128, d), f32),
             pltpu.VMEM((3, 2, 64, d), f32),
             dma((4, 2 * PIECES)), dma((3, STEPS)), dma((3,)), dma((3,)),
-            dma((3, 2)), dma((4, 2)), dma, dma, dma((4, 2)),
+            dma((3, 2)), dma((4, 2)), dma, dma, dma, dma((PIECES,)),
         ],
         compiler_params=pltpu.CompilerParams(
             collective_id=0, has_side_effects=True, vmem_limit_bytes=60 * 2**20
         ),
         cost_estimate=pl.CostEstimate(
-            flops=2 * tokens * ff * d, bytes_accessed=2 * ff * (d + tokens), transcendentals=0
+            flops=4 * tokens * ff * d, bytes_accessed=4 * ff * d, transcendentals=0
         ),
     )(upstream, bin_fill, activations.T, weight)
-    tile = 1024
     d_weight = pl.pallas_call(
-        functools.partial(weight_kernel, ff // 256),
+        weight_kernel,
         out_shape=jax.ShapeDtypeStruct((d, ff), bf16),
-        grid=(pl.cdiv(ff, tile),),
-        in_specs=[
-            pl.BlockSpec((d, tokens), lambda i: (0, 0)),
-            pl.BlockSpec((tokens, tile), lambda i: (0, i)),
+        in_specs=[hbm] * 3,
+        out_specs=hbm,
+        scratch_shapes=[
+            pltpu.VMEM((d, tokens), bf16),
+            pltpu.VMEM((4, 128, ff), bf16),
+            pltpu.VMEM((d, ff), bf16),
+            dma, dma((PIECES,)), dma((PIECES,)),
         ],
-        out_specs=pl.BlockSpec((d, tile), lambda i: (0, i)),
-        compiler_params=pltpu.CompilerParams(vmem_limit_bytes=58 * 2**20),
+        compiler_params=pltpu.CompilerParams(vmem_limit_bytes=60 * 2**20),
         cost_estimate=pl.CostEstimate(
-            flops=2 * tokens * ff * d, bytes_accessed=2 * ff * (d + tokens), transcendentals=0
+            flops=tokens * ff * d, bytes_accessed=4 * ff * d, transcendentals=0
         ),
-    )(act_t, gathered)
+    )(dw_head, gathered, act_t)
     return d_input.T, d_weight
 
 

time: 108 us -> 298 us (2.76)
  Pallas kernels: 105 us -> 295 us
    pallas_call x2, Pallas kernels: 105 us -> 295 us  [the longest x1 203 us: fused(): pl.pallas_call(weight_kernel, out_shape=jax.ShapeDtypeStruct((d, ff), bf1...]
where the time goes in v3:
time: 298 us; the launch traced here: 297 us
  Pallas kernels  295 us (99%)
    pallas_call x1, Pallas kernels, fused(): pl.pallas_call(weight_kernel, out_shape=jax.ShapeDtypeStruct((d, ff), bf1...  203 us
    pallas_call x1, Pallas kernels, fused(): pl.pallas_call(gather_kernel, out_shape=(jax.ShapeDtypeStruct((d, ff), bf...  92.7 us

profile of v3, /device:TPU:1, one launch (start us, length us, event | category | flops | bytes accessed | tf_op | source)
XLA Modules:
  0.0 297.4 jit_solution(11992528218991930601)
XLA Ops:
  1.3 92.7 %shard_map.59 = (bf16[928,7424]{1,0:T(8,128)(2,1)}, bf16[4,128,7424]{2,1,0:T(8,128)(2,1)}, bf16[928,512]{1,0:T(8,128)(2,1)}, bf16[928,128]{1,0:T(8,128)(2,1)}) custom-call(bf16[64,7424]{1,0:T(8,128)(2,1)} %up_ref.1, s32[1]{0:T(128)S(6)} %copy.7.fill_ref, bf16[928,128]{1,0:T(8,128)(2,1)} %bitcast.3, bf16[928,7424]{1,0:T(8,128)(2,1)} %w_ref.1), custom_call_target="tpu_custom_call" | custom-call | flops 14109638656 | bytes 27557888 | tf_op jit(solution)/shard_map/pallas_call | solution.py:284
  94.0 0.0 copy-start
  94.0 202.8 %shard_map.60 = bf16[928,7424]{1,0:T(8,128)(2,1)} custom-call(bf16[928,7424]{1,0:T(8,128)(2,1)} %get-tuple-element.7.dw_ref, bf16[4,128,7424]{2,1,0:T(8,128)(2,1)} %get-tuple-element.8.g_ref, bf16[928,512]{1,0:T(8,128)(2,1)} %get-tuple-element.9.act_ref), custom_call_target="tpu_custom_call" | custom-call | flops 3527409664 | bytes 27557888 | tf_op jit(solution)/shard_map/pallas_call | solution.py:313
  296.7 0.0 copy-done
  296.8 0.7 copy.8
Async XLA Ops:
  94.0 202.8 %copy-start = (bf16[928,128]{1,0:T(8,128)(2,1)S(1)}, bf16[928,128]{1,0:T(8,128)(2,1)}, u32[]{:S(2)}) copy-start(bf16[928,128]{1,0:T(8,128)(2,1)} %get-tuple-element.6) | copy-start | bytes 712708

commit v4 on v3

--- a/solution.py
+++ b/solution.py
@@ -254,22 +254,24 @@
         i: pltpu.make_async_copy(g_ref.at[:, :, columns[i]], gv.at[:, :, columns[i]], in_sem.at[i])
         for i in TAIL
     }
+    head = [i for i in ALL if i not in TAIL]
+    for i in head:
+        loads[i] = pltpu.make_async_copy(
+            dw_ref.at[:, columns[i]], dw.at[:, columns[i]], in_sem.at[i]
+        )
     for load in loads.values():
         load.start()
     saves = {
-        i: pltpu.make_async_copy(
-            (dw if i in TAIL else dw_ref).at[:, columns[i]], out_ref.at[:, columns[i]], out_sem.at[i]
-        )
+        i: pltpu.make_async_copy(dw.at[:, columns[i]], out_ref.at[:, columns[i]], out_sem.at[i])
         for i in ALL
     }
-    for i in ALL:
-        if i not in TAIL:
-            saves[i].start()
     load_act.wait()
-    for i in TAIL:
+    for i, j in zip(TAIL, head):
         loads[i].wait()
         weight_columns(act, gv, dw, cut[i], cut[i + 1])
         saves[i].start()
+        loads[j].wait()
+        saves[j].start()
     for i in ALL:
         saves[i].wait()
 

time: 298 us -> 107 us (0.36)
  Pallas kernels: 295 us -> 105 us
    pallas_call x1, Pallas kernels: 203 us -> 11.9 us  [fused(): pl.pallas_call(weight_kernel, out_shape=jax.ShapeDtypeStruct((d, ff), bf1...]
where the time goes in v4:
time: 107 us
  Pallas kernels  105 us (98%)
  between operations  1.31 us (1%)
    pallas_call x1, Pallas kernels, fused(): pl.pallas_call(gather_kernel, out_shape=(jax.ShapeDtypeStruct((d, ff), bf...  92.7 us
    pallas_call x1, Pallas kernels, fused(): pl.pallas_call(weight_kernel, out_shape=jax.ShapeDtypeStruct((d, ff), bf1...  11.9 us

profile of v4, /device:TPU:1, one launch (start us, length us, event | category | flops | bytes accessed | tf_op | source)
XLA Modules:
  0.0 106.6 jit_solution(1071516821081098601)
XLA Ops:
  1.3 92.7 %shard_map.59 = (bf16[928,7424]{1,0:T(8,128)(2,1)}, bf16[4,128,7424]{2,1,0:T(8,128)(2,1)}, bf16[928,512]{1,0:T(8,128)(2,1)}, bf16[928,128]{1,0:T(8,128)(2,1)}) custom-call(bf16[64,7424]{1,0:T(8,128)(2,1)} %up_ref.1, s32[1]{0:T(128)S(6)} %copy.7.fill_ref, bf16[928,128]{1,0:T(8,128)(2,1)} %bitcast.3, bf16[928,7424]{1,0:T(8,128)(2,1)} %w_ref.1), custom_call_target="tpu_custom_call" | custom-call | flops 14109638656 | bytes 27557888 | tf_op jit(solution)/shard_map/pallas_call | solution.py:286
  94.0 0.0 copy-start
  94.0 11.9 %shard_map.60 = bf16[928,7424]{1,0:T(8,128)(2,1)} custom-call(bf16[928,7424]{1,0:T(8,128)(2,1)} %get-tuple-element.7.dw_ref, bf16[4,128,7424]{2,1,0:T(8,128)(2,1)} %get-tuple-element.8.g_ref, bf16[928,512]{1,0:T(8,128)(2,1)} %get-tuple-element.9.act_ref), custom_call_target="tpu_custom_call" | custom-call | flops 3527409664 | bytes 27557888 | tf_op jit(solution)/shard_map/pallas_call | solution.py:315
  105.9 0.0 copy-done
  105.9 0.7 copy.8
Async XLA Ops:
  94.0 12.0 %copy-start = (bf16[928,128]{1,0:T(8,128)(2,1)S(1)}, bf16[928,128]{1,0:T(8,128)(2,1)}, u32[]{:S(2)}) copy-start(bf16[928,128]{1,0:T(8,128)(2,1)} %get-tuple-element.6) | copy-start | bytes 712708

commit v5 on v4

--- a/solution.py
+++ b/solution.py
@@ -10,7 +10,7 @@
 MESH = pl.DeviceIdType.MESH
 PIECES = 8
 STEPS = 28
-WINDOW = 3
+WINDOW = 5
 
 
 ALL = tuple(range(PIECES))

time: 107 us -> 107 us (level)
  no operation moved by 1% of the time
where the time goes in v5:
time: 107 us
  Pallas kernels  105 us (98%)
  between operations  1.31 us (1%)
    pallas_call x1, Pallas kernels, fused(): pl.pallas_call(gather_kernel, out_shape=(jax.ShapeDtypeStruct((d, ff), bf...  92.7 us
    pallas_call x1, Pallas kernels, fused(): pl.pallas_call(weight_kernel, out_shape=jax.ShapeDtypeStruct((d, ff), bf1...  11.9 us

profile of v5, /device:TPU:1, one launch (start us, length us, event | category | flops | bytes accessed | tf_op | source)
XLA Modules:
  0.0 106.7 jit_solution(821686136264029265)
XLA Ops:
  1.3 92.7 %shard_map.59 = (bf16[928,7424]{1,0:T(8,128)(2,1)}, bf16[4,128,7424]{2,1,0:T(8,128)(2,1)}, bf16[928,512]{1,0:T(8,128)(2,1)}, bf16[928,128]{1,0:T(8,128)(2,1)}) custom-call(bf16[64,7424]{1,0:T(8,128)(2,1)} %up_ref.1, s32[1]{0:T(128)S(6)} %copy.7.fill_ref, bf16[928,128]{1,0:T(8,128)(2,1)} %bitcast.3, bf16[928,7424]{1,0:T(8,128)(2,1)} %w_ref.1), custom_call_target="tpu_custom_call" | custom-call | flops 14109638656 | bytes 27557888 | tf_op jit(solution)/shard_map/pallas_call | solution.py:286
  94.0 0.0 copy-start
  94.0 11.9 %shard_map.60 = bf16[928,7424]{1,0:T(8,128)(2,1)} custom-call(bf16[928,7424]{1,0:T(8,128)(2,1)} %get-tuple-element.7.dw_ref, bf16[4,128,7424]{2,1,0:T(8,128)(2,1)} %get-tuple-element.8.g_ref, bf16[928,512]{1,0:T(8,128)(2,1)} %get-tuple-element.9.act_ref), custom_call_target="tpu_custom_call" | custom-call | flops 3527409664 | bytes 27557888 | tf_op jit(solution)/shard_map/pallas_call | solution.py:315
  106.0 0.0 copy-done
  106.0 0.7 copy.8
Async XLA Ops:
  94.0 12.0 %copy-start = (bf16[928,128]{1,0:T(8,128)(2,1)S(1)}, bf16[928,128]{1,0:T(8,128)(2,1)}, u32[]{:S(2)}) copy-start(bf16[928,128]{1,0:T(8,128)(2,1)} %get-tuple-element.6) | copy-start | bytes 712708
